TPU v7x, 128 devices: a whole 4x4x4 slice. The times are simulated.
128 devices in a mesh: rb: 16 (over z, y_lo, core), cb: 8 (over x, y_hi).
Axes of the slice: x: 4, y: 4 (y_hi: 2, y_lo: 2; y = y_hi * 2 + y_lo), z: 4, core: 2. Of those that a mesh axis runs over, the one named last changes fastest.
Arguments:
- pair_map: float32 [512, 512, 128], P(('rb', 'cb')), may hold values from -6 to 6
- norm_gain_start: float32 [128], replicated, may hold values from 0.1 to 1.9
- norm_shift_start: float32 [128], replicated, may hold values from -3 to 3
- proj_start: bfloat16 [128, 512], replicated, may hold values from -16 to 16
- bias_weight_start: bfloat16 [128, 4], replicated, may hold values from -1 to 1
- gate_bias_start: float32 [128], replicated, may hold values from -4 to 4
- out_weight_start: bfloat16 [128, 128], replicated, may hold values from -0.5 to 0.5
- out_bias_start: float32 [128], replicated, may hold values from -3 to 3
- norm_gain_end: float32 [128], replicated, may hold values from 0.1 to 1.9
- norm_shift_end: float32 [128], replicated, may hold values from -3 to 3
- proj_end: bfloat16 [128, 512], replicated, may hold values from -16 to 16
- bias_weight_end: bfloat16 [128, 4], replicated, may hold values from -1 to 1
- gate_bias_end: float32 [128], replicated, may hold values from -4 to 4
- out_weight_end: bfloat16 [128, 128], replicated, may hold values from -0.5 to 0.5
- out_bias_end: float32 [128], replicated, may hold values from -3 to 3
Outputs:
- updated_pair: float32 [512, 512, 128], P(('rb', 'cb'))
All inputs are finite; a program needn't handle non-finite values.
Results may differ from a plain program's by a relative error of at most 0.0065.
The roundings to bfloat16 on the way count: a program that leaves them out, or rounds other values in their place, can miss the bound.
Values may be sent and summed in bfloat16 or wider, within the bound.
A program may use at most 64 MiB of HBM per device.

v0:
```python
import jax
import jax.numpy as jnp
from jax import lax
from jax.sharding import PartitionSpec as P

H = 4
HEAD = 32


def layer_norm(pair, gain, shift):
    mean = jnp.mean(pair, axis=-1, keepdims=True)
    varia = jnp.mean((pair - mean) ** 2, axis=-1, keepdims=True)
    return ((pair - mean) / jnp.sqrt(varia + 1e-05) * gain + shift).astype(jnp.bfloat16)


def project(normed, proj, gate_bias):
    width = H * HEAD
    rows, length, chans = normed.shape
    projected = jnp.dot(
        normed.reshape(rows * length, chans), proj, preferred_element_type=jnp.float32
    )
    query = (
        (projected[:, :width] / jnp.sqrt(jnp.float32(HEAD)))
        .astype(jnp.bfloat16)
        .reshape(rows, length, H, HEAD)
    )
    keys = projected[:, width : 2 * width].astype(jnp.bfloat16).reshape(rows, length, H, HEAD)
    values = projected[:, 2 * width : 3 * width].astype(jnp.bfloat16).reshape(rows, length, H, HEAD)
    gate = jax.nn.sigmoid(projected[:, 3 * width :] + gate_bias).reshape(rows, length, width)
    return (query, keys, values, gate)


def row_bias(normed, bias_weight):
    return jnp.einsum(
        "jkc,ch->jhk", normed, bias_weight, preferred_element_type=jnp.float32
    ).astype(jnp.bfloat16)


def make_attention(tensors, piece):
    query, keys, values, gate = tensors
    width = H * HEAD
    count = piece.shape[0]
    bias_wide = piece.astype(jnp.float32)

    def one_row(args):
        row_q, row_k, row_v, row_g = args
        scores = (
            jnp.einsum("jhc,khc->jhk", row_q, row_k, preferred_element_type=jnp.float32) + bias_wide
        )
        weights = jax.nn.softmax(scores, axis=-1).astype(jnp.bfloat16)
        attended = jnp.einsum(
            "jhk,khc->jhc", weights, row_v, preferred_element_type=jnp.float32
        ).reshape(count, width)
        return (row_g * attended).astype(jnp.bfloat16)

    return lax.map(one_row, (query, keys, values, gate))


def finish(pair, gated, out_weight, out_bias):
    rows, length, chans = pair.shape
    update = jnp.dot(
        gated.reshape(rows * length, gated.shape[-1]),
        out_weight,
        preferred_element_type=jnp.float32,
    )
    return pair + update.reshape(rows, length, chans) + out_bias


def flip_rows(block):
    rows, length, chans = block.shape
    flat = block.reshape(1, rows, length, chans)
    moved = lax.all_to_all(flat, ("rb", "cb"), split_axis=2, concat_axis=0, tiled=True)
    return jnp.transpose(moved.reshape(length, rows, chans), (1, 0, 2))


def body(
    pair_map,
    norm_gain_start,
    norm_shift_start,
    proj_start,
    bias_weight_start,
    gate_bias_start,
    out_weight_start,
    out_bias_start,
    norm_gain_end,
    norm_shift_end,
    proj_end,
    bias_weight_end,
    gate_bias_end,
    out_weight_end,
    out_bias_end,
):
    normed = layer_norm(pair_map, norm_gain_start, norm_shift_start)
    tensors = project(normed, proj_start, gate_bias_start)
    bias_local = row_bias(normed, bias_weight_start)
    gated = make_attention(tensors, lax.all_gather(bias_local, ("rb", "cb"), axis=0, tiled=True))
    after_start = finish(pair_map, gated, out_weight_start, out_bias_start)
    flipped = None
    flipped = flip_rows(after_start)
    normed_end = layer_norm(flipped, norm_gain_end, norm_shift_end)
    tensors_end = project(normed_end, proj_end, gate_bias_end)
    bias_end = row_bias(normed_end, bias_weight_end)
    gated_end = make_attention(
        tensors_end, lax.all_gather(bias_end, ("rb", "cb"), axis=0, tiled=True)
    )
    ended = finish(flipped, gated_end, out_weight_end, out_bias_end)
    return flip_rows(ended)


def solution(mesh):
    in_specs = (
        P(("rb", "cb"), None, None),
        P(),
        P(),
        P(),
        P(),
        P(),
        P(),
        P(),
        P(),
        P(),
        P(),
        P(),
        P(),
        P(),
        P(),
    )
    out_specs = P(("rb", "cb"), None, None)
    return jax.shard_map(body, mesh=mesh, in_specs=in_specs, out_specs=out_specs, check_vma=False)
```

profile of v0, /device:TPU:1, one launch (start us, length us, event | category | flops | bytes accessed | tf_op | source)
XLA Modules:
  0.0 809.6 jit_solution(12718236057862866566)
XLA Ops:
  20.9 297.4 %all-gather.3.cloned.1.call-done = bf16[512,4,512]{2,1,0:T(4,128)(2,1)} async-done(((bf16[4,4,512]{2,1,0:T(4,128)(2,1)}), bf16[512,4,512]{2,1,0:T(4,128)(2,1)}) %all-gather.3.cloned.1.call-update) | async-done | bytes 2097168 | tf_op jit(solution)/shard_map/all_gather | solution.py:96
  318.3 4.8 copy.59
  323.9 56.4 %while.20 = (s32[]{:T(128)}, bf16[4,512,128]{1,2,0:T(8,128)(2,1)}, f32[4,512,128]{2,1,0:T(8,128)S(1)}, bf16[4,512,4,32]{1,3,2,0:T(8,128)(2,1)}, bf16[4,512,4,32]...) while((s32[]{:T(128)}, bf16[4,512,128]{1,2,0:T(8,128)(2,1)}, ...), condition=%wide.region_5.6_spmd, body=%wide.region_2.5_spmd.sunk | while | flops 208800768 | bytes 23612504 | solution.py:56
  324.0 5.1 bitcast_add_fusion.4
  329.0 3.6 fusion.98
  332.6 4.6 fusion.99
  338.1 5.0 bitcast_add_fusion.4
  343.1 3.6 fusion.98
  346.7 4.6 fusion.99
  352.2 5.0 bitcast_add_fusion.4
  357.2 3.6 fusion.98
  360.8 4.6 fusion.99
  366.2 5.0 bitcast_add_fusion.4
  371.2 3.6 fusion.98
  374.9 4.6 fusion.99
  382.4 27.8 %all_to_all.30 = f32[1,4,512,128]{3,1,0,2:T(4,128)S(1)} all-to-all(f32[1,4,512,128]{3,1,0,2:T(4,128)S(1)} %copy.61), channel_id=1, replica_groups=mesh['rb'=16,'cb'=8] {'rb','cb'}, dimensions={2} | all-to-all | bytes 2097152 | tf_op jit(solution)/shard_map/all_to_all | solution.py:72
  429.1 280.7 %all-gather.5.cloned.1.call-done = bf16[512,4,512]{2,1,0:T(4,128)(2,1)} async-done(((bf16[4,4,512]{2,1,0:T(4,128)(2,1)}), bf16[512,4,512]{2,1,0:T(4,128)(2,1)}) %all-gather.5.cloned.1.call-update) | async-done | bytes 2097168 | tf_op jit(solution)/shard_map/all_gather | solution.py:104
  709.8 4.8 copy.70
  715.5 56.3 %while.21 = (s32[]{:T(128)}, bf16[4,512,128]{1,2,0:T(8,128)(2,1)}, f32[4,512,128]{2,1,0:T(8,128)S(1)}, bf16[4,512,4,32]{1,3,2,0:T(8,128)(2,1)}, bf16[4,512,4,32]...) while((s32[]{:T(128)}, bf16[4,512,128]{1,2,0:T(8,128)(2,1)}, ...), condition=%wide.region_11.12_spmd, body=%wide.region_8.11_spmd.sunk | while | flops 208800768 | bytes 23612504 | solution.py:56
  715.5 5.0 bitcast_add_fusion.5
  720.5 3.6 fusion.106
  724.1 4.6 fusion.107
  729.6 5.0 bitcast_add_fusion.5
  734.5 3.6 fusion.106
  738.2 4.6 fusion.107
  743.6 5.0 bitcast_add_fusion.5
  748.6 3.6 fusion.106
  752.2 4.6 fusion.107
  757.7 5.0 bitcast_add_fusion.5
  762.7 3.6 fusion.106
  766.3 4.6 fusion.107
  773.9 27.7 %all_to_all.31 = f32[1,4,512,128]{3,1,0,2:T(4,128)S(1)} all-to-all(f32[1,4,512,128]{3,1,0,2:T(4,128)S(1)} %copy.72), channel_id=1, replica_groups=mesh['rb'=16,'cb'=8] {'rb','cb'}, dimensions={2} | all-to-all | bytes 2097152 | tf_op jit(solution)/shard_map/all_to_all | solution.py:72
  (92 shorter events, 46.8 us)
Async XLA Ops:
  6.5 6.9 copy-start
  6.5 311.7 %all-gather.3.cloned.1.call-start = ((), (), s32[]{:S(2)}) async-start(), calls=%async_computation.2 | async-start | bytes 2113536 | tf_op jit(solution)/shard_map/all_gather | solution.py:96
  10.0 5.5 copy-start.8
  13.4 696.4 %all-gather.5.cloned.1.call-start = ((), (), s32[]{:S(2)}) async-start(), calls=%async_computation.3 | async-start | bytes 2113536 | tf_op jit(solution)/shard_map/all_gather | solution.py:104
  323.9 56.4 %copy-start.1 = (f32[4,512,128]{2,1,0:T(8,128)S(1)}, f32[4,512,128]{2,1,0:T(8,128)}, u32[]{:S(2)}) copy-start(f32[4,512,128]{2,1,0:T(8,128)} %param.19) | copy-start | bytes 3145732
  323.9 56.4 %copy-start.4 = (f32[128]{0:T(128)S(1)}, f32[128]{0:T(128)}, u32[]{:S(2)}) copy-start(f32[128]{0:T(128)} %param.26) | copy-start | bytes 1540
  381.7 29.7 %copy-start.5 = (f32[128]{0:T(128)S(1)}, f32[128]{0:T(128)}, u32[]{:S(2)}) copy-start(f32[128]{0:T(128)} %param.28) | copy-start | bytes 1540
  381.7 29.7 %copy-start.6 = (f32[128]{0:T(128)S(1)}, f32[128]{0:T(128)}, u32[]{:S(2)}) copy-start(f32[128]{0:T(128)} %param.27) | copy-start | bytes 1540
  382.4 29.8 %copy-start.3 = (bf16[128,4]{0,1:T(4,128)(2,1)S(1)}, bf16[128,4]{0,1:T(4,128)(2,1)}, u32[]{:S(2)}) copy-start(bf16[128,4]{0,1:T(4,128)(2,1)} %param.30) | copy-start | bytes 3076
  382.4 30.7 %copy-start.2 = (bf16[128,512]{1,0:T(8,128)(2,1)S(1)}, bf16[128,512]{1,0:T(8,128)(2,1)}, u32[]{:S(2)}) copy-start(bf16[128,512]{1,0:T(8,128)(2,1)} %param.29) | copy-start | bytes 393220
  411.5 3.7 copy-start.9
  715.5 56.3 %copy-start.7 = (f32[128]{0:T(128)S(1)}, f32[128]{0:T(128)}, u32[]{:S(2)}) copy-start(f32[128]{0:T(128)} %param.33) | copy-start | bytes 1540
Sparse Core Ops, SparseCore 0:
  13.5 304.6 all-gather.2
  413.2 296.5 all-gather.4
where the time goes:
time: 811 us; the launch traced here: 810 us
  waiting for transfers between devices  578 us (71%)
  matrix products  115 us (14%)
  blocking collectives  55.5 us (7%)
  local copies, waits for them, and re-layouts  34 us (4%)
  between operations  13.7 us (2%)
  other arithmetic  13.1 us (2%)
    all_gather x1, waiting for transfers between devices, body(): lax.all_gather(bias_local, ('rb', 'cb'), axis=0, tiled=True)  297 us
    all_gather x1, waiting for transfers between devices, body(): lax.all_gather(bias_end, ('rb', 'cb'), axis=0, tiled=True)  281 us
    all_to_all x2, blocking collectives, flip_rows(): lax.all_to_all(flat, ('rb', 'cb'), split_axis=2, concat_axis=0, tiled=True)  55.5 us
    dot_general x8, matrix products, one_row(): jnp.einsum('jhc,khc->jhk', row_q, row_k, preferred_element_type=jnp.float32)  40 us
    dot_general x8, matrix products, one_row(): jnp.einsum('jhk,khc->jhc', weights, row_v, preferred_element_type=jnp.flo...  36.8 us
    sub x8, matrix products, one_row(): weights = jax.nn.softmax(scores, axis=-1).astype(jnp.bfloat16)  28.9 us
    while x8, local copies, waits for them, and re-layouts, make_attention(): return lax.map(one_row, (query, keys, values, gate))  16.8 us
  transfers between devices with their start and end apart: 2, of which 2 were waited for; matrix products, arithmetic and copies ran while one was open for 3% of the time, Pallas kernels for 0%

commit v1 on v0

v1 whole, which is shorter than its diff:
```python
import functools

import jax
import jax.numpy as jnp
from jax import lax
from jax.experimental import pallas as pl
from jax.experimental.pallas import tpu as pltpu
from jax.sharding import PartitionSpec as P

H = 4
HEAD = 32
WIDTH = H * HEAD
ROWS = 4
N = 512
C = 128
DEV = 128
MESH = pl.DeviceIdType.MESH
f32 = jnp.float32
bf16 = jnp.bfloat16

ORDERS = (("x", "y", "z"), ("y", "z", "x"), ("z", "x", "y"), ("x", "z", "y"))


def where_am_i():
    rb, cb = lax.axis_index("rb"), lax.axis_index("cb")
    return {
        "z": rb // 4,
        "y": (cb % 2) * 2 + (rb // 2) % 2,
        "x": cb // 2,
        "core": rb % 2,
    }


def device_of(at):
    return (at["z"] * 4 + (at["y"] % 2) * 2 + at["core"], at["x"] * 2 + at["y"] // 2)


def slot_y(y):
    return (y % 2) * 2 + y // 2


def slot_of(at):
    return at["z"] * 32 + slot_y(at["y"]) * 8 + at["x"] * 2 + at["core"]


def shifted(at, axis, by):
    size = 2 if axis == "core" else 4
    return {**at, axis: (at[axis] + by) % size}


def perms():
    row = lax.broadcasted_iota(jnp.int32, (256, 256), 0)
    col = lax.broadcasted_iota(jnp.int32, (256, 256), 1)

    def slot(n):
        return (n % 2) * 8 + ((n // 2) % 4) * 2 + n // 8

    a, n, b = row // 64, (row // 4) % 16, row % 4
    to_rows = jnp.where(col == slot(n) * 16 + a * 4 + b, 1.0, 0.0).astype(bf16)
    a, n, b = col // 64, (col // 4) % 16, col % 4
    to_slots = jnp.where(row == slot(n) * 16 + b * 4 + a, 1.0, 0.0).astype(bf16)
    return to_rows, to_slots


def layer_norm(pair, gain, shift):
    mean = jnp.mean(pair, axis=-1, keepdims=True)
    away = pair - mean
    varia = jnp.mean(away * away, axis=-1, keepdims=True)
    return (away / jnp.sqrt(varia + 1e-05) * gain + shift).astype(bf16)


def bias_slab(normed_ref, bias_weight):
    pick = lax.broadcasted_iota(jnp.int32, (16, H), 0) // 4 == lax.broadcasted_iota(jnp.int32, (16, H), 1)
    wide = lax.dot_general(
        jnp.where(pick, 1.0, 0.0).astype(bf16), bias_weight, (((1,), (1,)), ((), ())), preferred_element_type=f32
    )
    row = lax.broadcasted_iota(jnp.int32, (16, C), 0) % 4
    total = jnp.zeros((16, N), f32)
    for j in range(ROWS):
        mine = jnp.where(row == j, wide, 0.0).astype(bf16)
        total += lax.dot_general(mine, normed_ref[j], (((1,), (1,)), ((), ())), preferred_element_type=f32)
    return total.astype(bf16)


def gather_copy(bias, at, chunk, phase, by, send_sem, recv_sem):
    z, y, x, core = at["z"], slot_y(at["y"]), at["x"], at["core"]
    lanes = pl.ds(chunk * 128, 128)
    done = ("x", "y", "z") if phase == 3 else ORDERS[chunk][:phase]
    axis = "core" if phase == 3 else ORDERS[chunk][phase]
    all4 = pl.ds(0, 4)
    part = bias.at[
        all4 if "z" in done else z,
        all4 if "y" in done else y,
        all4 if "x" in done else x,
        core,
        :,
        lanes,
    ]
    return pltpu.make_async_remote_copy(
        src_ref=part,
        dst_ref=part,
        send_sem=send_sem.at[chunk, phase, by - 1],
        recv_sem=recv_sem.at[chunk, phase, by - 1],
        device_id=device_of(shifted(at, axis, by)),
        device_id_type=MESH,
    )


def offsets(phase):
    return (1,) if phase == 3 else (1, 2, 3)


def gather_start(bias, at, phase, send_sem, recv_sem):
    for chunk in range(4):
        if phase > 0:
            for by in offsets(phase - 1):
                gather_copy(bias, at, chunk, phase - 1, by, send_sem, recv_sem).wait_recv()
        for by in offsets(phase):
            gather_copy(bias, at, chunk, phase, by, send_sem, recv_sem).start()


def gather_end(bias, at, send_sem, recv_sem):
    for chunk in range(4):
        gather_copy(bias, at, chunk, 3, 1, send_sem, recv_sem).wait_recv()


def gather_drain(bias, at, send_sem, recv_sem):
    for phase in range(4):
        for chunk in range(4):
            for by in offsets(phase):
                gather_copy(bias, at, chunk, phase, by, send_sem, recv_sem).wait_send()


def spread_bias(bias, wide, to_rows):
    for z in range(4):
        for y in range(2):
            slabs = bias[z, 2 * y : 2 * y + 2].reshape(256, N)
            rows = jnp.dot(to_rows, slabs, preferred_element_type=f32)
            first = (z * 2 + y) * 64
            for h in range(H):
                wide[h, first : first + 64, :] = rows[h * 64 : (h + 1) * 64]


def projections(normed_ref, proj, gate_bias, query, keys, values, gate):
    for i in range(ROWS):
        out = jnp.dot(normed_ref[i], proj, preferred_element_type=f32)
        query[i] = (out[:, :WIDTH] / jnp.sqrt(f32(HEAD))).astype(bf16)
        keys[i] = out[:, WIDTH : 2 * WIDTH].astype(bf16)
        values[i] = out[:, 2 * WIDTH : 3 * WIDTH].astype(bf16)
        gate[i] = jax.nn.sigmoid(out[:, 3 * WIDTH :] + gate_bias)


def head_lanes(h, shape):
    return lax.broadcasted_iota(jnp.int32, shape, len(shape) - 1) // HEAD == h


def attention_row(i, query, keys, values, gate, wide):
    q, k, v = query[i], keys[i], values[i]
    total = None
    for h in range(H):
        lanes = head_lanes(h, (N, C))
        q_h = jnp.where(lanes, q, 0.0).astype(bf16)
        scores = lax.dot_general(q_h, k, (((1,), (1,)), ((), ())), preferred_element_type=f32) + wide[h]
        top = jnp.max(scores, axis=-1, keepdims=True)
        weights = jnp.exp(scores - top).astype(bf16)
        v_h = jnp.concatenate(
            [jnp.where(lanes, v, 0.0).astype(bf16), jnp.where(lanes, 1.0, 0.0).astype(bf16)], axis=1
        )
        part = jnp.dot(weights, v_h, preferred_element_type=f32)
        total = part if total is None else total + part
    return (gate[i] * (total[:, :WIDTH] / total[:, WIDTH:])).astype(bf16)


def exchange(at, send, recv, send_sem, recv_sem):
    me = slot_of(at)
    recv[me] = send[me]

    def start(o, carry):
        to = {
            "z": (at["z"] + o // 32) % 4,
            "y": (at["y"] + (o // 8) % 4) % 4,
            "x": (at["x"] + (o // 2) % 4) % 4,
            "core": (at["core"] + o % 2) % 2,
        }
        pltpu.make_async_remote_copy(
            src_ref=send.at[slot_of(to)],
            dst_ref=recv.at[me],
            send_sem=send_sem,
            recv_sem=recv_sem,
            device_id=device_of(to),
            device_id_type=MESH,
        ).start()
        return carry

    lax.fori_loop(1, DEV, start, 0)
    others = pl.ds(0, DEV - 1)
    whole = pltpu.make_async_remote_copy(
        src_ref=send.at[others],
        dst_ref=recv.at[others],
        send_sem=send_sem,
        recv_sem=recv_sem,
        device_id=device_of(shifted(at, "core", 1)),
        device_id_type=MESH,
    )
    whole.wait_recv()
    whole.wait_send()


def to_send(rows, send, to_slots):
    for g in range(8):
        part = jnp.concatenate([rows[i, g * 64 : (g + 1) * 64, :] for i in range(ROWS)], axis=0)
        moved = jnp.dot(to_slots, part, preferred_element_type=f32).astype(bf16)
        send[g * 16 : (g + 1) * 16] = moved.reshape(16, 16, C)


def from_recv(recv, rows, to_rows):
    for g in range(8):
        part = recv[g * 16 : (g + 1) * 16].reshape(256, C)
        moved = jnp.dot(to_rows, part, preferred_element_type=f32).astype(bf16)
        for i in range(ROWS):
            rows[i, g * 64 : (g + 1) * 64, :] = moved[i * 64 : (i + 1) * 64]


def kernel(
    pair,
    gain_s, shift_s, proj_s, bias_weight_s, gate_bias_s, out_weight_s, out_bias_s,
    gain_e, shift_e, proj_e, bias_weight_e, gate_bias_e, out_weight_e, out_bias_e,
    out,
    normed, query, keys, values, gate, wide, rows,
    bias_s, bias_e, send_a, recv_a, send_b, recv_b,
    g_send_s, g_recv_s, g_send_e, g_recv_e, x_send, x_recv,
):
    at = where_am_i()
    barrier = pltpu.get_barrier_semaphore()
    greet = [shifted(at, axis, by) for axis in ("x", "y", "z") for by in (1, 2, 3)] + [shifted(at, "core", 1)]
    for other in greet:
        pl.semaphore_signal(barrier, inc=1, device_id=device_of(other), device_id_type=MESH)

    z, y, x, core = at["z"], slot_y(at["y"]), at["x"], at["core"]
    to_rows, to_slots = perms()
    vec = lambda ref: ref[...].reshape(1, C)

    def norm_row(i, carry):
        normed[i] = layer_norm(pair[i], vec(gain_s), vec(shift_s))
        return carry

    lax.fori_loop(0, ROWS, norm_row, 0)
    bias_s[z, y, x, core] = bias_slab(normed, bias_weight_s[...])
    pl.semaphore_wait(barrier, len(greet))
    gather_start(bias_s, at, 0, g_send_s, g_recv_s)
    projections(normed, proj_s[...], vec(gate_bias_s), query, keys, values, gate)
    for phase in (1, 2, 3):
        gather_start(bias_s, at, phase, g_send_s, g_recv_s)
    gather_end(bias_s, at, g_send_s, g_recv_s)
    spread_bias(bias_s, wide, to_rows)

    def start_row(i, carry):
        gated = attention_row(i, query, keys, values, gate, wide)
        update = jnp.dot(gated, out_weight_s[...], preferred_element_type=f32)
        after = pair[i] + update + vec(out_bias_s)
        out[i] = after
        rows[i] = layer_norm(after, vec(gain_e), vec(shift_e))
        return carry

    lax.fori_loop(0, ROWS, start_row, 0)
    to_send(rows, send_a, to_slots)
    exchange(at, send_a, recv_a, x_send.at[0], x_recv.at[0])
    from_recv(recv_a, normed, to_rows)

    bias_e[z, y, x, core] = bias_slab(normed, bias_weight_e[...])
    gather_start(bias_e, at, 0, g_send_e, g_recv_e)
    projections(normed, proj_e[...], vec(gate_bias_e), query, keys, values, gate)
    for phase in (1, 2, 3):
        gather_start(bias_e, at, phase, g_send_e, g_recv_e)
    gather_end(bias_e, at, g_send_e, g_recv_e)
    spread_bias(bias_e, wide, to_rows)

    def end_row(i, carry):
        rows[i] = attention_row(i, query, keys, values, gate, wide)
        return carry

    lax.fori_loop(0, ROWS, end_row, 0)
    to_send(rows, send_b, to_slots)
    exchange(at, send_b, recv_b, x_send.at[1], x_recv.at[1])
    from_recv(recv_b, rows, to_rows)

    def finish_row(i, carry):
        update = jnp.dot(rows[i], out_weight_e[...], preferred_element_type=f32)
        out[i] = out[i] + update + vec(out_bias_e)
        return carry

    lax.fori_loop(0, ROWS, finish_row, 0)
    gather_drain(bias_s, at, g_send_s, g_recv_s)
    gather_drain(bias_e, at, g_send_e, g_recv_e)


def body(*args):
    vmem = pl.BlockSpec(memory_space=pltpu.VMEM)
    slab = (4, 4, 4, 2, 16, N)
    return pl.pallas_call(
        kernel,
        out_shape=jax.ShapeDtypeStruct((ROWS, N, C), f32),
        in_specs=[vmem] * len(args),
        out_specs=vmem,
        scratch_shapes=[
            pltpu.VMEM((ROWS, N, C), bf16),
            pltpu.VMEM((ROWS, N, C), bf16),
            pltpu.VMEM((ROWS, N, C), bf16),
            pltpu.VMEM((ROWS, N, C), bf16),
            pltpu.VMEM((ROWS, N, C), f32),
            pltpu.VMEM((H, N, N), f32),
            pltpu.VMEM((ROWS, N, C), bf16),
            pltpu.VMEM(slab, bf16),
            pltpu.VMEM(slab, bf16),
            pltpu.VMEM((DEV, 16, C), bf16),
            pltpu.VMEM((DEV, 16, C), bf16),
            pltpu.VMEM((DEV, 16, C), bf16),
            pltpu.VMEM((DEV, 16, C), bf16),
            pltpu.SemaphoreType.DMA((4, 4, 3)),
            pltpu.SemaphoreType.DMA((4, 4, 3)),
            pltpu.SemaphoreType.DMA((4, 4, 3)),
            pltpu.SemaphoreType.DMA((4, 4, 3)),
            pltpu.SemaphoreType.DMA((2,)),
            pltpu.SemaphoreType.DMA((2,)),
        ],
        compiler_params=pltpu.CompilerParams(
            collective_id=0, has_side_effects=True, vmem_limit_bytes=56 << 20
        ),
    )(*args)


def solution(mesh):
    rows = P(("rb", "cb"), None, None)
    return jax.shard_map(body, mesh=mesh, in_specs=(rows,) + (P(),) * 14, out_specs=rows, check_vma=False)
```

time: 811 us -> 88.4 us (0.11)
  waiting for transfers between devices: 578 us -> 0 us
  matrix products: 115 us -> 0 us
  Pallas kernels: 0 us -> 83.8 us
  blocking collectives: 55.5 us -> 0 us
  local copies, waits for them, and re-layouts: 34 us -> 4.42 us
  between operations: 13.7 us -> 0.01 us
  other arithmetic: 13.1 us -> 0 us
    all_gather x2 -> x0, waiting for transfers between devices: 578 us -> none  [the longest x1 297 us: body(): lax.all_gather(bias_local, ('rb', 'cb'), axis=0, tiled=True)]
    dot_general x22 -> x0, matrix products: 86 us -> none  [the longest x8 40 us: one_row(): jnp.einsum('jhc,khc->jhk', row_q, row_k, preferred_element_type=jnp.float32)]
    pallas_call x0 -> x1, Pallas kernels: none -> 83.8 us  [body(): pl.pallas_call(kernel, out_shape=jax.ShapeDtypeStruct((ROWS, N, C), f32),...]
    all_to_all x2 -> x0, blocking collectives: 55.5 us -> none  [flip_rows(): lax.all_to_all(flat, ('rb', 'cb'), split_axis=2, concat_axis=0, tiled=True)]
    sub x8 -> x0, matrix products: 28.9 us -> none  [one_row(): weights = jax.nn.softmax(scores, axis=-1).astype(jnp.bfloat16)]
    while x8 -> x0, local copies, waits for them, and re-layouts: 16.8 us -> none  [make_attention(): return lax.map(one_row, (query, keys, values, gate))]
  transfers between devices with their start and end apart: 2 -> 0, of which waited for: 2 -> 0; matrix products, arithmetic and copies ran while one was open for 3% -> 0% of each run, Pallas kernels for 0% -> 0%
where the time goes in v1:
time: 88.4 us; the launch traced here: 88.2 us
  Pallas kernels  83.8 us (95%)
  local copies, waits for them, and re-layouts  4.42 us (5%)
    pallas_call x1, Pallas kernels, body(): pl.pallas_call(kernel, out_shape=jax.ShapeDtypeStruct((ROWS, N, C), f32),...  83.8 us
    unnamed x5, local copies, waits for them, and re-layouts  4.42 us

profile of v1, /device:TPU:1, one launch (start us, length us, event | category | flops | bytes accessed | tf_op | source)
XLA Modules:
  0.0 88.2 jit_solution(10615390670243248809)
XLA Ops:
  0.0 0.0 copy-start
  0.0 1.4 %copy.16.bias_weight_s = bf16[128,4]{1,0:T(8,128)(2,1)} copy(bf16[128,4]{0,1:T(4,128)(2,1)} %param.19) | data formatting | bytes 2048 | tf_op args[4]
  1.4 0.0 copy-done
  1.4 0.7 copy.17.bias_weight_e
  2.2 83.8 %shard_map.145 = f32[4,512,128]{2,1,0:T(8,128)} custom-call(f32[4,512,128]{2,1,0:T(8,128)} %pair.1, f32[128]{0:T(128)} %gain_s.1, f32[128]{0:T(128)} %shift_s.1, bf16[128,512]{1,0:T(8,128)(2,1)} %proj_s.1, bf16[128,4]{1,0:T(8,128)(2,1)} %copy.16.bias_weight_s, f32[128]{0:T(128)} %gate_bias_s.1, bf16[128,128]{1,0:T(8,128)(2,1)} %out_weight_s.1, ...), custom_call_target="tpu_custom_call" | custom-call | tf_op jit(solution)/shard_map/pallas_call | solution.py:300
  86.0 2.3 %copy.19 = f32[4,512,128]{2,1,0:T(8,128)} copy(f32[4,512,128]{2,1,0:T(8,128)} %shard_map.145) | data formatting | bytes 2097152
Async XLA Ops:
  0.0 1.4 %copy-start = (bf16[128,4]{0,1:T(4,128)(2,1)S(1)}, bf16[128,4]{0,1:T(4,128)(2,1)}, u32[]{:S(2)}) copy-start(bf16[128,4]{0,1:T(4,128)(2,1)} %param.26) | copy-start | bytes 3076

commit v2 on v1

v2 whole, which is shorter than its diff:
```python
import functools

import jax
import jax.numpy as jnp
from jax import lax
from jax.experimental import pallas as pl
from jax.experimental.pallas import tpu as pltpu
from jax.sharding import PartitionSpec as P

H = 4
HEAD = 32
WIDTH = H * HEAD
ROWS = 4
N = 512
C = 128
DEV = 128
MESH = pl.DeviceIdType.MESH
f32 = jnp.float32
bf16 = jnp.bfloat16

LINES = ("z", "x", "y", "z")
STEPS = (2, 1, 3, 0)


def where_am_i():
    rb, cb = lax.axis_index("rb"), lax.axis_index("cb")
    return {
        "z": rb // 4,
        "y": (cb % 2) * 2 + (rb // 2) % 2,
        "x": cb // 2,
        "core": rb % 2,
    }


def device_of(at):
    return (at["z"] * 4 + (at["y"] % 2) * 2 + at["core"], at["x"] * 2 + at["y"] // 2)


def slot_y(y):
    return (y % 2) * 2 + y // 2


def slot_of(at):
    return at["z"] * 32 + slot_y(at["y"]) * 8 + at["x"] * 2 + at["core"]


def shifted(at, axis, by):
    size = 2 if axis == "core" else 4
    return {**at, axis: (at[axis] + by) % size}


def perms():
    row = lax.broadcasted_iota(jnp.int32, (256, 256), 0)
    col = lax.broadcasted_iota(jnp.int32, (256, 256), 1)

    def slot(n):
        return (n % 2) * 8 + ((n // 2) % 4) * 2 + n // 8

    a, n, b = row // 64, (row // 4) % 16, row % 4
    to_rows = jnp.where(col == slot(n) * 16 + a * 4 + b, 1.0, 0.0).astype(bf16)
    a, n, b = col // 64, (col // 4) % 16, col % 4
    to_slots = jnp.where(row == slot(n) * 16 + b * 4 + a, 1.0, 0.0).astype(bf16)
    return to_rows, to_slots


def lane_perm():
    row = lax.broadcasted_iota(jnp.int32, (512, 512), 0)
    col = lax.broadcasted_iota(jnp.int32, (512, 512), 1)
    a, n, b = col // 128, (col // 4) % 32, col % 4
    slot = n // 16 * 16 + (n % 2) * 8 + ((n // 2) % 4) * 2 + (n // 8) % 2
    return jnp.where(row == slot * 16 + a * 4 + b, 1.0, 0.0).astype(bf16)


def layer_norm(pair, gain, shift):
    mean = jnp.mean(pair, axis=-1, keepdims=True)
    away = pair - mean
    varia = jnp.mean(away * away, axis=-1, keepdims=True)
    return (away / jnp.sqrt(varia + 1e-05) * gain + shift).astype(bf16)


def bias_slab(normed, bias_rows):
    pick = lax.broadcasted_iota(jnp.int32, (16, H), 0) // 4 == lax.broadcasted_iota(jnp.int32, (16, H), 1)
    wide = jnp.dot(jnp.where(pick, 1.0, 0.0).astype(bf16), bias_rows, preferred_element_type=f32)
    row = lax.broadcasted_iota(jnp.int32, (16, C), 0) % 4
    total = None
    for i in range(ROWS):
        mine = jnp.where(row == i, wide, 0.0).astype(bf16)
        part = lax.dot_general(mine, normed[i], (((1,), (1,)), ((), ())), preferred_element_type=f32)
        total = part if total is None else total + part
    return total.astype(bf16)


def tiles(ref, count):
    return ref.at[pl.ds(0, count)]


def wait_for(ref, count, at, send_sem, recv_sem, sent):
    part = tiles(ref, count)
    copy = pltpu.make_async_remote_copy(
        src_ref=part,
        dst_ref=part,
        send_sem=send_sem,
        recv_sem=recv_sem,
        device_id=device_of(shifted(at, "core", 1)),
        device_id_type=MESH,
    )
    if sent:
        copy.wait_send()
    else:
        copy.wait_recv()


def part_of(bias, at, chunk, whole):
    all4 = pl.ds(0, 4)
    return bias.at[
        all4 if "z" in whole else at["z"],
        all4 if "y" in whole else slot_y(at["y"]),
        all4 if "x" in whole else at["x"],
        at["core"],
        :,
        pl.ds(chunk * 128, 128),
    ]


def push(part, to, send_sem, recv_sem):
    pltpu.make_async_remote_copy(
        src_ref=part,
        dst_ref=part,
        send_sem=send_sem,
        recv_sem=recv_sem,
        device_id=device_of(to),
        device_id_type=MESH,
    ).start()


def plane_of(chunk):
    return [axis for axis in ("z", "y", "x") if axis != LINES[chunk]]


def plane_peers(at, chunk):
    first, second = plane_of(chunk)
    for one in (2, 1, 3, 0):
        for two in (2, 1, 3, 0):
            if one or two:
                yield shifted(shifted(at, first, one), second, two)


def gather_plane(bias, at, chunk, send_sem, recv_sem):
    part = part_of(bias, at, chunk, ())
    for to in plane_peers(at, chunk):
        push(part, to, send_sem.at[chunk, 0], recv_sem.at[chunk, 0])


def gather_line(bias, at, chunk, send_sem, recv_sem, spare):
    wait_for(spare, 15, at, send_sem.at[chunk, 0], recv_sem.at[chunk, 0], False)
    part = part_of(bias, at, chunk, plane_of(chunk))
    for by in (2, 1, 3):
        push(part, shifted(at, LINES[chunk], by), send_sem.at[chunk, 1], recv_sem.at[chunk, 1])


def gather_core(bias, at, chunk, send_sem, recv_sem, spare):
    wait_for(spare, 48, at, send_sem.at[chunk, 1], recv_sem.at[chunk, 1], False)
    push(part_of(bias, at, chunk, ("z", "y", "x")), shifted(at, "core", 1), send_sem.at[chunk, 2], recv_sem.at[chunk, 2])


def gather_end(at, chunk, send_sem, recv_sem, spare):
    wait_for(spare, 64, at, send_sem.at[chunk, 2], recv_sem.at[chunk, 2], False)


def gather_drain(at, send_sem, recv_sem, spare):
    for chunk in range(4):
        for phase, count in ((0, 15), (1, 48), (2, 64)):
            wait_for(spare, count, at, send_sem.at[chunk, phase], recv_sem.at[chunk, phase], True)


def spread_start(bias, wide, to_rows):
    for z in range(4):
        for y in range(2):
            slabs = bias[z, 2 * y : 2 * y + 2].reshape(256, N)
            rows = jnp.dot(to_rows, slabs, preferred_element_type=f32)
            for h in range(H):
                first = h * 128 + y * 64
                wide[z, first : first + 64, :] = rows[h * 64 : (h + 1) * 64]


def spread_end(bias, wide, to_lanes):
    for z in range(4):
        for step in range(4):
            block = (z + STEPS[step]) % 4
            slabs = bias[z, :, :, :, :, step * 128 : (step + 1) * 128].reshape(512, 128)
            cols = lax.dot_general(slabs, to_lanes, (((0,), (0,)), ((), ())), preferred_element_type=f32)
            for h in range(H):
                wide[block, h * 128 : (h + 1) * 128, z * 128 : (z + 1) * 128] = cols[:, h * 128 : (h + 1) * 128]


def projections(normed_ref, proj, gate_bias, query, keys, values, gate):
    for i in range(ROWS):
        out = jnp.dot(normed_ref[i], proj, preferred_element_type=f32)
        query[i] = (out[:, :WIDTH] / jnp.sqrt(f32(HEAD))).astype(bf16)
        keys[i] = out[:, WIDTH : 2 * WIDTH].astype(bf16)
        values[i] = out[:, 2 * WIDTH : 3 * WIDTH].astype(bf16)
        gate[i] = jax.nn.sigmoid(out[:, 3 * WIDTH :] + gate_bias)


def head_lanes(h, shape):
    return lax.broadcasted_iota(jnp.int32, shape, len(shape) - 1) // HEAD == h


def attention_block(i, first, wide, query, keys, values, gate):
    here = pl.ds(first, 128)
    lanes = [head_lanes(h, (128, C)) for h in range(H)]
    q = query[i, here, :]
    q_heads = jnp.concatenate([jnp.where(lane, q, 0.0).astype(bf16) for lane in lanes], axis=0)
    scores = lax.dot_general(q_heads, keys[i], (((1,), (1,)), ((), ())), preferred_element_type=f32) + wide
    top = jnp.max(scores, axis=-1, keepdims=True)
    weights = jnp.exp(scores - top).astype(bf16)
    v_ones = jnp.concatenate([values[i], jnp.ones((N, C), bf16)], axis=1)
    sums = jnp.dot(weights, v_ones, preferred_element_type=f32)

    def own_head(cols):
        parts = [sums[h * 128 : (h + 1) * 128, cols : cols + WIDTH] for h in range(H)]
        return jnp.where(lanes[0], parts[0], jnp.where(lanes[1], parts[1], jnp.where(lanes[2], parts[2], parts[3])))

    return (gate[i, here, :] * (own_head(0) / own_head(WIDTH))).astype(bf16)


def send_block(at, step, block, blocks, send, recv, to_slots, send_sem, recv_sem):
    for g in range(2):
        part = jnp.concatenate([rows[g * 64 : (g + 1) * 64] for rows in blocks], axis=0)
        moved = jnp.dot(to_slots, part, preferred_element_type=f32).astype(bf16)
        send[pl.ds(block * 32 + g * 16, 16)] = moved.reshape(16, 16, C)
    me = slot_of(at)

    def start(o, carry):
        q = 31 - o
        to = {
            "z": block,
            "y": (at["y"] + q // 8) % 4,
            "x": (at["x"] + (q // 2) % 4) % 4,
            "core": (at["core"] + q % 2) % 2,
        }
        pltpu.make_async_remote_copy(
            src_ref=send.at[slot_of(to)],
            dst_ref=recv.at[me],
            send_sem=send_sem,
            recv_sem=recv_sem,
            device_id=device_of(to),
            device_id_type=MESH,
        ).start()
        return carry

    lax.fori_loop(0, 31, start, 0)

    @pl.when(step < 3)
    def _():
        start(31, 0)

    @pl.when(step == 3)
    def _():
        recv[me] = send[me]


def from_recv(recv, rows, to_rows):
    for g in range(8):
        part = recv[g * 16 : (g + 1) * 16].reshape(256, C)
        moved = jnp.dot(to_rows, part, preferred_element_type=f32).astype(bf16)
        for i in range(ROWS):
            rows[i, g * 64 : (g + 1) * 64, :] = moved[i * 64 : (i + 1) * 64]


def block_of(at, step):
    by = jnp.where(step == 0, STEPS[0], jnp.where(step == 1, STEPS[1], jnp.where(step == 2, STEPS[2], STEPS[3])))
    return (at["z"] + by) % 4


def kernel(
    pair,
    gain_s, shift_s, proj_s, bias_rows_s, gate_bias_s, out_weight_s, out_bias_s,
    gain_e, shift_e, proj_e, bias_rows_e, gate_bias_e, out_weight_e, out_bias_e,
    out,
    normed, query, keys, values, gate, wide, to_lanes,
    bias_s, bias_e, send_a, recv_a, send_b, recv_b,
    g_send_s, g_recv_s, g_send_e, g_recv_e, x_send, x_recv,
):
    at = where_am_i()
    barrier = pltpu.get_barrier_semaphore()
    greet = [shifted(at, axis, by) for axis in ("x", "y", "z") for by in (1, 2, 3)] + [shifted(at, "core", 1)]
    for one, two in (("x", "y"), ("x", "z"), ("y", "z")):
        greet += [shifted(shifted(at, one, i), two, j) for i in (1, 2, 3) for j in (1, 2, 3)]
    for other in greet:
        pl.semaphore_signal(barrier, inc=1, device_id=device_of(other), device_id_type=MESH)

    z, y, x, core = at["z"], slot_y(at["y"]), at["x"], at["core"]
    vec = lambda ref: ref[...].reshape(1, C)

    def norm_row(i, carry):
        normed[i] = layer_norm(pair[i], vec(gain_s), vec(shift_s))
        return carry

    lax.fori_loop(0, ROWS, norm_row, 0)
    bias_s[z, y, x, core] = bias_slab(normed, bias_rows_s[...])
    pl.semaphore_wait(barrier, len(greet))
    for chunk in range(4):
        gather_plane(bias_s, at, chunk, g_send_s, g_recv_s)
    projections(normed, proj_s[...], vec(gate_bias_s), query, keys, values, gate)
    to_rows, to_slots = perms()
    to_lanes[...] = lane_perm()
    for chunk in range(4):
        gather_line(bias_s, at, chunk, g_send_s, g_recv_s, recv_a)
    for chunk in range(4):
        gather_core(bias_s, at, chunk, g_send_s, g_recv_s, recv_a)
    for chunk in range(4):
        gather_end(at, chunk, g_send_s, g_recv_s, recv_a)
    spread_start(bias_s, wide, to_rows)

    def start_step(step, carry):
        block = block_of(at, step)
        first = pl.multiple_of(block * 128, 128)
        blocks = []
        for i in range(ROWS):
            gated = attention_block(i, first, wide[block], query, keys, values, gate)
            update = jnp.dot(gated, out_weight_s[...], preferred_element_type=f32)
            after = pair[i, pl.ds(first, 128), :] + update + vec(out_bias_s)
            out[i, pl.ds(first, 128), :] = after
            blocks.append(layer_norm(after, vec(gain_e), vec(shift_e)))
        slab = bias_slab(blocks, bias_rows_e[...])
        for s in range(4):

            @pl.when(step == s)
            def _(s=s):
                bias_e[z, y, x, core, :, s * 128 : (s + 1) * 128] = slab
                gather_plane(bias_e, at, s, g_send_e, g_recv_e)
                if s >= 2:
                    gather_line(bias_e, at, s - 2, g_send_e, g_recv_e, recv_b)

        send_block(at, step, block, blocks, send_a, recv_a, to_slots, x_send.at[0], x_recv.at[0])
        return carry

    lax.fori_loop(0, 4, start_step, 0)
    for chunk in (2, 3):
        gather_line(bias_e, at, chunk, g_send_e, g_recv_e, recv_b)
    for chunk in (0, 1):
        gather_core(bias_e, at, chunk, g_send_e, g_recv_e, recv_b)
    wait_for(recv_a, DEV - 1, at, x_send.at[0], x_recv.at[0], False)
    from_recv(recv_a, normed, to_rows)
    projections(normed, proj_e[...], vec(gate_bias_e), query, keys, values, gate)
    for chunk in (2, 3):
        gather_core(bias_e, at, chunk, g_send_e, g_recv_e, recv_b)
    for chunk in range(4):
        gather_end(at, chunk, g_send_e, g_recv_e, recv_b)
    spread_end(bias_e, wide, to_lanes[...])

    def end_step(step, carry):
        block = block_of(at, step)
        first = pl.multiple_of(block * 128, 128)
        blocks = [attention_block(i, first, wide[block], query, keys, values, gate) for i in range(ROWS)]
        send_block(at, step, block, blocks, send_b, recv_b, to_slots, x_send.at[1], x_recv.at[1])
        return carry

    lax.fori_loop(0, 4, end_step, 0)
    gather_drain(at, g_send_s, g_recv_s, recv_a)
    gather_drain(at, g_send_e, g_recv_e, recv_a)
    wait_for(recv_b, DEV - 1, at, x_send.at[1], x_recv.at[1], False)
    from_recv(recv_b, normed, to_rows)

    def finish_row(i, carry):
        update = jnp.dot(normed[i], out_weight_e[...], preferred_element_type=f32)
        out[i] = out[i] + update + vec(out_bias_e)
        return carry

    lax.fori_loop(0, ROWS, finish_row, 0)
    for trip in range(2):
        wait_for(recv_a, DEV - 1, at, x_send.at[trip], x_recv.at[trip], True)


def body(*args):
    args = [arg.T if arg.shape == (C, H) else arg for arg in args]
    vmem = pl.BlockSpec(memory_space=pltpu.VMEM)
    slab = (4, 4, 4, 2, 16, N)
    return pl.pallas_call(
        kernel,
        out_shape=jax.ShapeDtypeStruct((ROWS, N, C), f32),
        in_specs=[vmem] * len(args),
        out_specs=vmem,
        scratch_shapes=[
            pltpu.VMEM((ROWS, N, C), bf16),
            pltpu.VMEM((ROWS, N, C), bf16),
            pltpu.VMEM((ROWS, N, C), bf16),
            pltpu.VMEM((ROWS, N, C), bf16),
            pltpu.VMEM((ROWS, N, C), f32),
            pltpu.VMEM((4, H * 128, N), f32),
            pltpu.VMEM((512, 512), bf16),
            pltpu.VMEM(slab, bf16),
            pltpu.VMEM(slab, bf16),
            pltpu.VMEM((DEV, 16, C), bf16),
            pltpu.VMEM((DEV, 16, C), bf16),
            pltpu.VMEM((DEV, 16, C), bf16),
            pltpu.VMEM((DEV, 16, C), bf16),
            pltpu.SemaphoreType.DMA((4, 3)),
            pltpu.SemaphoreType.DMA((4, 3)),
            pltpu.SemaphoreType.DMA((4, 3)),
            pltpu.SemaphoreType.DMA((4, 3)),
            pltpu.SemaphoreType.DMA((2,)),
            pltpu.SemaphoreType.DMA((2,)),
        ],
        compiler_params=pltpu.CompilerParams(
            collective_id=0, has_side_effects=True, vmem_limit_bytes=56 << 20
        ),
    )(*args)


def solution(mesh):
    rows = P(("rb", "cb"), None, None)
    return jax.shard_map(body, mesh=mesh, in_specs=(rows,) + (P(),) * 14, out_specs=rows, check_vma=False)
```

time: 88.4 us -> 73.8 us (0.83)
  Pallas kernels: 83.8 us -> 71.3 us
  local copies, waits for them, and re-layouts: 4.42 us -> 2.26 us
    pallas_call x1, Pallas kernels: 83.8 us -> 71.3 us  [body(): pl.pallas_call(kernel, out_shape=jax.ShapeDtypeStruct((ROWS, N, C), f32),...]
    unnamed x5 -> x1, local copies, waits for them, and re-layouts: 4.42 us -> 2.26 us
where the time goes in v2:
time: 73.8 us; the launch traced here: 73.6 us
  Pallas kernels  71.3 us (97%)
  local copies, waits for them, and re-layouts  2.26 us (3%)
    pallas_call x1, Pallas kernels, body(): pl.pallas_call(kernel, out_shape=jax.ShapeDtypeStruct((ROWS, N, C), f32),...  71.3 us
    unnamed x1, local copies, waits for them, and re-layouts  2.26 us

profile of v2, /device:TPU:1, one launch (start us, length us, event | category | flops | bytes accessed | tf_op | source)
XLA Modules:
  0.0 73.6 jit_solution(4616444715437089054)
XLA Ops:
  0.0 71.3 %shard_map.145 = f32[4,512,128]{2,1,0:T(8,128)} custom-call(f32[4,512,128]{2,1,0:T(8,128)} %pair.1, f32[128]{0:T(128)} %gain_s.1, f32[128]{0:T(128)} %shift_s.1, bf16[128,512]{1,0:T(8,128)(2,1)} %proj_s.1, bf16[4,128]{1,0:T(4,128)(2,1)} %bitcast.2, f32[128]{0:T(128)} %gate_bias_s.1, bf16[128,128]{1,0:T(8,128)(2,1)} %out_weight_s.1, f32[128]{0:T(128)} %out_bias_s.1, ...), custom_call_target="tpu_custom_call" | custom-call | tf_op jit(solution)/shard_map/pallas_call | solution.py:380
  71.3 2.3 %copy.17 = f32[4,512,128]{2,1,0:T(8,128)} copy(f32[4,512,128]{2,1,0:T(8,128)} %shard_map.145) | data formatting | bytes 2097152

commit v3 on v2

--- a/solution.py
+++ b/solution.py
@@ -173,45 +173,50 @@
             wait_for(spare, count, at, send_sem.at[chunk, phase], recv_sem.at[chunk, phase], True)
 
 
-def spread_start(bias, wide, to_rows):
+def spread_start(bias, wide, to_rows, chunk):
+    here = slice(chunk * 128, (chunk + 1) * 128)
     for z in range(4):
         for y in range(2):
-            slabs = bias[z, 2 * y : 2 * y + 2].reshape(256, N)
+            slabs = bias[z, 2 * y : 2 * y + 2, :, :, :, here].reshape(256, 128)
             rows = jnp.dot(to_rows, slabs, preferred_element_type=f32)
             for h in range(H):
                 first = h * 128 + y * 64
-                wide[z, first : first + 64, :] = rows[h * 64 : (h + 1) * 64]
-
-
-def spread_end(bias, wide, to_lanes):
+                wide[z, first : first + 64, here] = rows[h * 64 : (h + 1) * 64]
+
+
+def spread_end(bias, wide, to_lanes, step):
     for z in range(4):
-        for step in range(4):
-            block = (z + STEPS[step]) % 4
-            slabs = bias[z, :, :, :, :, step * 128 : (step + 1) * 128].reshape(512, 128)
-            cols = lax.dot_general(slabs, to_lanes, (((0,), (0,)), ((), ())), preferred_element_type=f32)
-            for h in range(H):
-                wide[block, h * 128 : (h + 1) * 128, z * 128 : (z + 1) * 128] = cols[:, h * 128 : (h + 1) * 128]
-
-
-def projections(normed_ref, proj, gate_bias, query, keys, values, gate):
-    for i in range(ROWS):
-        out = jnp.dot(normed_ref[i], proj, preferred_element_type=f32)
-        query[i] = (out[:, :WIDTH] / jnp.sqrt(f32(HEAD))).astype(bf16)
-        keys[i] = out[:, WIDTH : 2 * WIDTH].astype(bf16)
-        values[i] = out[:, 2 * WIDTH : 3 * WIDTH].astype(bf16)
-        gate[i] = jax.nn.sigmoid(out[:, 3 * WIDTH :] + gate_bias)
+        block = (z + STEPS[step]) % 4
+        slabs = bias[z, :, :, :, :, step * 128 : (step + 1) * 128].reshape(512, 128)
+        cols = lax.dot_general(slabs, to_lanes, (((0,), (0,)), ((), ())), preferred_element_type=f32)
+        for h in range(H):
+            wide[block, h * 128 : (h + 1) * 128, z * 128 : (z + 1) * 128] = cols[:, h * 128 : (h + 1) * 128]
+
+
+def project(i, here, rows, proj, gate_bias, query, keys, values, gate):
+    out = jnp.dot(rows, proj, preferred_element_type=f32)
+    query[i, here, :] = (out[:, :WIDTH] / jnp.sqrt(f32(HEAD))).astype(bf16)
+    keys[i, here, :] = out[:, WIDTH : 2 * WIDTH].astype(bf16)
+    values[i, here, :] = out[:, 2 * WIDTH : 3 * WIDTH].astype(bf16)
+    gate[i, here, :] = jax.nn.sigmoid(out[:, 3 * WIDTH :] + gate_bias)
 
 
 def head_lanes(h, shape):
     return lax.broadcasted_iota(jnp.int32, shape, len(shape) - 1) // HEAD == h
 
 
-def attention_block(i, first, wide, query, keys, values, gate):
-    here = pl.ds(first, 128)
+def pre_scores(block, query, keys, raw):
     lanes = [head_lanes(h, (128, C)) for h in range(H)]
-    q = query[i, here, :]
-    q_heads = jnp.concatenate([jnp.where(lane, q, 0.0).astype(bf16) for lane in lanes], axis=0)
-    scores = lax.dot_general(q_heads, keys[i], (((1,), (1,)), ((), ())), preferred_element_type=f32) + wide
+    for i in range(ROWS):
+        q = query[i, pl.ds(pl.multiple_of(block * 128, 128), 128), :]
+        q_heads = jnp.concatenate([jnp.where(lane, q, 0.0).astype(bf16) for lane in lanes], axis=0)
+        raw[block, i] = lax.dot_general(q_heads, keys[i], (((1,), (1,)), ((), ())), preferred_element_type=f32)
+
+
+def attention_block(i, block, raw, wide, values, gate):
+    here = pl.ds(pl.multiple_of(block * 128, 128), 128)
+    lanes = [head_lanes(h, (128, C)) for h in range(H)]
+    scores = raw[block, i] + wide[block]
     top = jnp.max(scores, axis=-1, keepdims=True)
     weights = jnp.exp(scores - top).astype(bf16)
     v_ones = jnp.concatenate([values[i], jnp.ones((N, C), bf16)], axis=1)
@@ -260,12 +265,12 @@
         recv[me] = send[me]
 
 
-def from_recv(recv, rows, to_rows):
-    for g in range(8):
-        part = recv[g * 16 : (g + 1) * 16].reshape(256, C)
-        moved = jnp.dot(to_rows, part, preferred_element_type=f32).astype(bf16)
-        for i in range(ROWS):
-            rows[i, g * 64 : (g + 1) * 64, :] = moved[i * 64 : (i + 1) * 64]
+def from_recv(recv, plane, to_rows):
+    halves = []
+    for g in range(2):
+        part = recv[pl.ds(plane * 32 + g * 16, 16)].reshape(256, C)
+        halves.append(jnp.dot(to_rows, part, preferred_element_type=f32).astype(bf16))
+    return [jnp.concatenate([half[i * 64 : (i + 1) * 64] for half in halves], axis=0) for i in range(ROWS)]
 
 
 def block_of(at, step):
@@ -274,13 +279,13 @@
 
 
 def kernel(
-    pair,
+    pair_hbm,
     gain_s, shift_s, proj_s, bias_rows_s, gate_bias_s, out_weight_s, out_bias_s,
     gain_e, shift_e, proj_e, bias_rows_e, gate_bias_e, out_weight_e, out_bias_e,
-    out,
-    normed, query, keys, values, gate, wide, to_lanes,
+    out_hbm,
+    pair, normed, query, keys, values, gate, wide, raw, to_lanes,
     bias_s, bias_e, send_a, recv_a, send_b, recv_b,
-    g_send_s, g_recv_s, g_send_e, g_recv_e, x_send, x_recv,
+    g_send_s, g_recv_s, g_send_e, g_recv_e, x_send, x_recv, in_sem, out_sem,
 ):
     at = where_am_i()
     barrier = pltpu.get_barrier_semaphore()
@@ -292,36 +297,41 @@
 
     z, y, x, core = at["z"], slot_y(at["y"]), at["x"], at["core"]
     vec = lambda ref: ref[...].reshape(1, C)
-
-    def norm_row(i, carry):
+    loads = [pltpu.make_async_copy(pair_hbm.at[i], pair.at[i], in_sem.at[i]) for i in range(ROWS)]
+    for load in loads:
+        load.start()
+    for i in range(ROWS):
+        loads[i].wait()
         normed[i] = layer_norm(pair[i], vec(gain_s), vec(shift_s))
-        return carry
-
-    lax.fori_loop(0, ROWS, norm_row, 0)
     bias_s[z, y, x, core] = bias_slab(normed, bias_rows_s[...])
     pl.semaphore_wait(barrier, len(greet))
     for chunk in range(4):
         gather_plane(bias_s, at, chunk, g_send_s, g_recv_s)
-    projections(normed, proj_s[...], vec(gate_bias_s), query, keys, values, gate)
+    for i in range(ROWS):
+        project(i, slice(None), normed[i], proj_s[...], vec(gate_bias_s), query, keys, values, gate)
+    for block in range(2):
+        pre_scores(block, query, keys, raw)
+    for chunk in range(4):
+        gather_line(bias_s, at, chunk, g_send_s, g_recv_s, recv_a)
+    for block in range(2, 4):
+        pre_scores(block, query, keys, raw)
     to_rows, to_slots = perms()
     to_lanes[...] = lane_perm()
     for chunk in range(4):
-        gather_line(bias_s, at, chunk, g_send_s, g_recv_s, recv_a)
-    for chunk in range(4):
         gather_core(bias_s, at, chunk, g_send_s, g_recv_s, recv_a)
     for chunk in range(4):
         gather_end(at, chunk, g_send_s, g_recv_s, recv_a)
-    spread_start(bias_s, wide, to_rows)
+        spread_start(bias_s, wide, to_rows, chunk)
 
     def start_step(step, carry):
         block = block_of(at, step)
-        first = pl.multiple_of(block * 128, 128)
+        here = pl.ds(pl.multiple_of(block * 128, 128), 128)
         blocks = []
         for i in range(ROWS):
-            gated = attention_block(i, first, wide[block], query, keys, values, gate)
+            gated = attention_block(i, block, raw, wide, values, gate)
             update = jnp.dot(gated, out_weight_s[...], preferred_element_type=f32)
-            after = pair[i, pl.ds(first, 128), :] + update + vec(out_bias_s)
-            out[i, pl.ds(first, 128), :] = after
+            after = pair[i, here, :] + update + vec(out_bias_s)
+            pair[i, here, :] = after
             blocks.append(layer_norm(after, vec(gain_e), vec(shift_e)))
         slab = bias_slab(blocks, bias_rows_e[...])
         for s in range(4):
@@ -333,44 +343,60 @@
                 if s >= 2:
                     gather_line(bias_e, at, s - 2, g_send_e, g_recv_e, recv_b)
 
-        send_block(at, step, block, blocks, send_a, recv_a, to_slots, x_send.at[0], x_recv.at[0])
+        send_block(at, step, block, blocks, send_a, recv_a, to_slots, x_send.at[0, step], x_recv.at[0, step])
         return carry
 
     lax.fori_loop(0, 4, start_step, 0)
-    for chunk in (2, 3):
-        gather_line(bias_e, at, chunk, g_send_e, g_recv_e, recv_b)
+
+    def receive(step):
+        plane = (z + 4 - STEPS[step]) % 4
+        wait_for(recv_a, 32 if step < 3 else 31, at, x_send.at[0, step], x_recv.at[0, step], False)
+        here = pl.ds(pl.multiple_of(plane * 128, 128), 128)
+        for i, rows in enumerate(from_recv(recv_a, plane, to_rows)):
+            project(i, here, rows, proj_e[...], vec(gate_bias_e), query, keys, values, gate)
+
+    receive(0)
+    receive(1)
+    gather_line(bias_e, at, 2, g_send_e, g_recv_e, recv_b)
+    receive(2)
+    gather_line(bias_e, at, 3, g_send_e, g_recv_e, recv_b)
     for chunk in (0, 1):
         gather_core(bias_e, at, chunk, g_send_e, g_recv_e, recv_b)
-    wait_for(recv_a, DEV - 1, at, x_send.at[0], x_recv.at[0], False)
-    from_recv(recv_a, normed, to_rows)
-    projections(normed, proj_e[...], vec(gate_bias_e), query, keys, values, gate)
-    for chunk in (2, 3):
-        gather_core(bias_e, at, chunk, g_send_e, g_recv_e, recv_b)
+    receive(3)
+    for block in range(2):
+        pre_scores(block, query, keys, raw)
+    gather_core(bias_e, at, 2, g_send_e, g_recv_e, recv_b)
+    for block in range(2, 4):
+        pre_scores(block, query, keys, raw)
+    gather_core(bias_e, at, 3, g_send_e, g_recv_e, recv_b)
     for chunk in range(4):
         gather_end(at, chunk, g_send_e, g_recv_e, recv_b)
-    spread_end(bias_e, wide, to_lanes[...])
+        spread_end(bias_e, wide, to_lanes[...], chunk)
 
     def end_step(step, carry):
         block = block_of(at, step)
-        first = pl.multiple_of(block * 128, 128)
-        blocks = [attention_block(i, first, wide[block], query, keys, values, gate) for i in range(ROWS)]
-        send_block(at, step, block, blocks, send_b, recv_b, to_slots, x_send.at[1], x_recv.at[1])
+        blocks = [attention_block(i, block, raw, wide, values, gate) for i in range(ROWS)]
+        send_block(at, step, block, blocks, send_b, recv_b, to_slots, x_send.at[1, step], x_recv.at[1, step])
         return carry
 
     lax.fori_loop(0, 4, end_step, 0)
     gather_drain(at, g_send_s, g_recv_s, recv_a)
     gather_drain(at, g_send_e, g_recv_e, recv_a)
-    wait_for(recv_b, DEV - 1, at, x_send.at[1], x_recv.at[1], False)
-    from_recv(recv_b, normed, to_rows)
-
-    def finish_row(i, carry):
-        update = jnp.dot(normed[i], out_weight_e[...], preferred_element_type=f32)
-        out[i] = out[i] + update + vec(out_bias_e)
-        return carry
-
-    lax.fori_loop(0, ROWS, finish_row, 0)
+    stores = []
+    for step in range(4):
+        plane = (z + 4 - STEPS[step]) % 4
+        here = pl.ds(pl.multiple_of(plane * 128, 128), 128)
+        wait_for(recv_b, 32 if step < 3 else 31, at, x_send.at[1, step], x_recv.at[1, step], False)
+        for i, rows in enumerate(from_recv(recv_b, plane, to_rows)):
+            update = jnp.dot(rows, out_weight_e[...], preferred_element_type=f32)
+            pair[i, here, :] = pair[i, here, :] + update + vec(out_bias_e)
+        stores.append(pltpu.make_async_copy(pair.at[:, here], out_hbm.at[:, here], out_sem.at[step]))
+        stores[-1].start()
     for trip in range(2):
-        wait_for(recv_a, DEV - 1, at, x_send.at[trip], x_recv.at[trip], True)
+        for step in range(4):
+            wait_for(recv_a, 32 if step < 3 else 31, at, x_send.at[trip, step], x_recv.at[trip, step], True)
+    for store in stores:
+        store.wait()
 
 
 def body(*args):
@@ -380,15 +406,17 @@
     return pl.pallas_call(
         kernel,
         out_shape=jax.ShapeDtypeStruct((ROWS, N, C), f32),
-        in_specs=[vmem] * len(args),
-        out_specs=vmem,
+        in_specs=[pl.BlockSpec(memory_space=pl.ANY)] + [vmem] * (len(args) - 1),
+        out_specs=pl.BlockSpec(memory_space=pl.ANY),
         scratch_shapes=[
+            pltpu.VMEM((ROWS, N, C), f32),
             pltpu.VMEM((ROWS, N, C), bf16),
             pltpu.VMEM((ROWS, N, C), bf16),
             pltpu.VMEM((ROWS, N, C), bf16),
             pltpu.VMEM((ROWS, N, C), bf16),
             pltpu.VMEM((ROWS, N, C), f32),
             pltpu.VMEM((4, H * 128, N), f32),
+            pltpu.VMEM((4, ROWS, H * 128, N), f32),
             pltpu.VMEM((512, 512), bf16),
             pltpu.VMEM(slab, bf16),
             pltpu.VMEM(slab, bf16),
@@ -400,8 +428,10 @@
             pltpu.SemaphoreType.DMA((4, 3)),
             pltpu.SemaphoreType.DMA((4, 3)),
             pltpu.SemaphoreType.DMA((4, 3)),
-            pltpu.SemaphoreType.DMA((2,)),
-            pltpu.SemaphoreType.DMA((2,)),
+            pltpu.SemaphoreType.DMA((2, 4)),
+            pltpu.SemaphoreType.DMA((2, 4)),
+            pltpu.SemaphoreType.DMA((4,)),
+            pltpu.SemaphoreType.DMA((4,)),
         ],
         compiler_params=pltpu.CompilerParams(
             collective_id=0, has_side_effects=True, vmem_limit_bytes=56 << 20

time: 73.8 us -> 66.7 us (0.904)
  Pallas kernels: 71.3 us -> 64.3 us
    pallas_call x1, Pallas kernels: 71.3 us -> 64.3 us  [body(): pl.pallas_call(kernel, out_shape=jax.ShapeDtypeStruct((ROWS, N, C), f32),...]
where the time goes in v3:
time: 66.7 us; the launch traced here: 66.5 us
  Pallas kernels  64.3 us (96%)
  local copies, waits for them, and re-layouts  2.26 us (3%)
    pallas_call x1, Pallas kernels, body(): pl.pallas_call(kernel, out_shape=jax.ShapeDtypeStruct((ROWS, N, C), f32),...  64.3 us
    unnamed x1, local copies, waits for them, and re-layouts  2.26 us

profile of v3, /device:TPU:1, one launch (start us, length us, event | category | flops | bytes accessed | tf_op | source)
XLA Modules:
  0.0 66.5 jit_solution(11749977549870036045)
XLA Ops:
  0.0 64.3 %shard_map.145 = f32[4,512,128]{2,1,0:T(8,128)} custom-call(f32[4,512,128]{2,1,0:T(8,128)} %pair_hbm.1, f32[128]{0:T(128)} %gain_s.1, f32[128]{0:T(128)} %shift_s.1, bf16[128,512]{1,0:T(8,128)(2,1)} %proj_s.1, bf16[4,128]{1,0:T(4,128)(2,1)} %bitcast.2, f32[128]{0:T(128)} %gate_bias_s.1, bf16[128,128]{1,0:T(8,128)(2,1)} %out_weight_s.1, f32[128]{0:T(128)} %out_bias_s.1, ...), custom_call_target="tpu_custom_call" | custom-call | tf_op jit(solution)/shard_map/pallas_call | solution.py:406
  64.3 2.3 %copy.17 = f32[4,512,128]{2,1,0:T(8,128)} copy(f32[4,512,128]{2,1,0:T(8,128)} %shard_map.145) | data formatting | bytes 2097152

commit v4 on v3

--- a/solution.py
+++ b/solution.py
@@ -18,7 +18,7 @@
 f32 = jnp.float32
 bf16 = jnp.bfloat16
 
-LINES = ("z", "x", "y", "z")
+LINES = (("z", "x", "y", "x"), ("z", "x", "y", "z"))
 STEPS = (2, 1, 3, 0)
 
 
@@ -133,43 +133,60 @@
     ).start()
 
 
-def plane_of(chunk):
-    return [axis for axis in ("z", "y", "x") if axis != LINES[chunk]]
-
-
-def plane_peers(at, chunk):
-    first, second = plane_of(chunk)
-    for one in (2, 1, 3, 0):
-        for two in (2, 1, 3, 0):
-            if one or two:
-                yield shifted(shifted(at, first, one), second, two)
+def along(at, chunk, act):
+    lines = [core_lines[chunk] for core_lines in LINES]
+    for core, line in enumerate(lines):
+        if core == 1 and lines[0] == lines[1]:
+            continue
+        plane = [axis for axis in ("z", "y", "x") if axis != line]
+        if lines[0] == lines[1]:
+            act(line, plane)
+        else:
+            pl.when(at["core"] == core)(functools.partial(act, line, plane))
 
 
 def gather_plane(bias, at, chunk, send_sem, recv_sem):
     part = part_of(bias, at, chunk, ())
-    for to in plane_peers(at, chunk):
-        push(part, to, send_sem.at[chunk, 0], recv_sem.at[chunk, 0])
+
+    def act(line, plane):
+        for one in (2, 1, 3, 0):
+            for two in (2, 1, 3, 0):
+                if one or two:
+                    to = shifted(shifted(at, plane[0], one), plane[1], two)
+                    push(part, to, send_sem.at[chunk, 0], recv_sem.at[chunk, 0])
+
+    along(at, chunk, act)
 
 
 def gather_line(bias, at, chunk, send_sem, recv_sem, spare):
     wait_for(spare, 15, at, send_sem.at[chunk, 0], recv_sem.at[chunk, 0], False)
-    part = part_of(bias, at, chunk, plane_of(chunk))
-    for by in (2, 1, 3):
-        push(part, shifted(at, LINES[chunk], by), send_sem.at[chunk, 1], recv_sem.at[chunk, 1])
+
+    def act(line, plane):
+        part = part_of(bias, at, chunk, plane)
+        for by in (2, 1, 3):
+            push(part, shifted(at, line, by), send_sem.at[chunk, by], recv_sem.at[chunk, by])
+        push(part, shifted(at, "core", 1), send_sem.at[chunk, 4], recv_sem.at[chunk, 4])
+
+    along(at, chunk, act)
 
 
 def gather_core(bias, at, chunk, send_sem, recv_sem, spare):
-    wait_for(spare, 48, at, send_sem.at[chunk, 1], recv_sem.at[chunk, 1], False)
-    push(part_of(bias, at, chunk, ("z", "y", "x")), shifted(at, "core", 1), send_sem.at[chunk, 2], recv_sem.at[chunk, 2])
+    def act(line, plane):
+        for by in (1, 3, 2):
+            wait_for(spare, 16, at, send_sem.at[chunk, by], recv_sem.at[chunk, by], False)
+            part = part_of(bias, shifted(at, line, 4 - by), chunk, plane)
+            push(part, shifted(at, "core", 1), send_sem.at[chunk, 4], recv_sem.at[chunk, 4])
+
+    along(at, chunk, act)
 
 
 def gather_end(at, chunk, send_sem, recv_sem, spare):
-    wait_for(spare, 64, at, send_sem.at[chunk, 2], recv_sem.at[chunk, 2], False)
+    wait_for(spare, 64, at, send_sem.at[chunk, 4], recv_sem.at[chunk, 4], False)
 
 
 def gather_drain(at, send_sem, recv_sem, spare):
     for chunk in range(4):
-        for phase, count in ((0, 15), (1, 48), (2, 64)):
+        for phase, count in ((0, 15), (1, 16), (2, 16), (3, 16), (4, 64)):
             wait_for(spare, count, at, send_sem.at[chunk, phase], recv_sem.at[chunk, phase], True)
 
 
@@ -236,14 +253,12 @@
         send[pl.ds(block * 32 + g * 16, 16)] = moved.reshape(16, 16, C)
     me = slot_of(at)
 
-    def start(o, carry):
-        q = 31 - o
-        to = {
-            "z": block,
-            "y": (at["y"] + q // 8) % 4,
-            "x": (at["x"] + (q // 2) % 4) % 4,
-            "core": (at["core"] + q % 2) % 2,
-        }
+    ys = [(at["y"] + by) % 4 for by in range(4)]
+    xs = [(at["x"] + by) % 4 for by in range(4)]
+    cores = [at["core"], 1 - at["core"]]
+
+    def start(q):
+        to = {"z": block, "y": ys[q // 8], "x": xs[q // 2 % 4], "core": cores[q % 2]}
         pltpu.make_async_remote_copy(
             src_ref=send.at[slot_of(to)],
             dst_ref=recv.at[me],
@@ -252,13 +267,13 @@
             device_id=device_of(to),
             device_id_type=MESH,
         ).start()
-        return carry
-
-    lax.fori_loop(0, 31, start, 0)
+
+    for q in range(31, 0, -1):
+        start(q)
 
     @pl.when(step < 3)
     def _():
-        start(31, 0)
+        start(0)
 
     @pl.when(step == 3)
     def _():
@@ -355,6 +370,10 @@
         for i, rows in enumerate(from_recv(recv_a, plane, to_rows)):
             project(i, here, rows, proj_e[...], vec(gate_bias_e), query, keys, values, gate)
 
+    def settle(chunk):
+        gather_end(at, chunk, g_send_e, g_recv_e, recv_b)
+        spread_end(bias_e, wide, to_lanes[...], chunk)
+
     receive(0)
     receive(1)
     gather_line(bias_e, at, 2, g_send_e, g_recv_e, recv_b)
@@ -366,12 +385,13 @@
     for block in range(2):
         pre_scores(block, query, keys, raw)
     gather_core(bias_e, at, 2, g_send_e, g_recv_e, recv_b)
+    settle(0)
+    settle(1)
     for block in range(2, 4):
         pre_scores(block, query, keys, raw)
     gather_core(bias_e, at, 3, g_send_e, g_recv_e, recv_b)
-    for chunk in range(4):
-        gather_end(at, chunk, g_send_e, g_recv_e, recv_b)
-        spread_end(bias_e, wide, to_lanes[...], chunk)
+    settle(2)
+    settle(3)
 
     def end_step(step, carry):
         block = block_of(at, step)
@@ -424,10 +444,10 @@
             pltpu.VMEM((DEV, 16, C), bf16),
             pltpu.VMEM((DEV, 16, C), bf16),
             pltpu.VMEM((DEV, 16, C), bf16),
-            pltpu.SemaphoreType.DMA((4, 3)),
-            pltpu.SemaphoreType.DMA((4, 3)),
-            pltpu.SemaphoreType.DMA((4, 3)),
-            pltpu.SemaphoreType.DMA((4, 3)),
+            pltpu.SemaphoreType.DMA((4, 5)),
+            pltpu.SemaphoreType.DMA((4, 5)),
+            pltpu.SemaphoreType.DMA((4, 5)),
+            pltpu.SemaphoreType.DMA((4, 5)),
             pltpu.SemaphoreType.DMA((2, 4)),
             pltpu.SemaphoreType.DMA((2, 4)),
             pltpu.SemaphoreType.DMA((4,)),

time: 66.7 us -> 63.6 us (0.954)
  Pallas kernels: 64.3 us -> 61.1 us
    pallas_call x1, Pallas kernels: 64.3 us -> 61.1 us  [body(): pl.pallas_call(kernel, out_shape=jax.ShapeDtypeStruct((ROWS, N, C), f32),...]
where the time goes in v4:
time: 63.6 us; the launch traced here: 63.4 us
  Pallas kernels  61.1 us (96%)
  local copies, waits for them, and re-layouts  2.26 us (4%)
    pallas_call x1, Pallas kernels, body(): pl.pallas_call(kernel, out_shape=jax.ShapeDtypeStruct((ROWS, N, C), f32),...  61.1 us
    unnamed x1, local copies, waits for them, and re-layouts  2.26 us

profile of v4, /device:TPU:1, one launch (start us, length us, event | category | flops | bytes accessed | tf_op | source)
XLA Modules:
  0.0 63.4 jit_solution(16533455079617387605)
XLA Ops:
  0.0 61.1 %shard_map.145 = f32[4,512,128]{2,1,0:T(8,128)} custom-call(f32[4,512,128]{2,1,0:T(8,128)} %pair_hbm.1, f32[128]{0:T(128)} %gain_s.1, f32[128]{0:T(128)} %shift_s.1, bf16[128,512]{1,0:T(8,128)(2,1)} %proj_s.1, bf16[4,128]{1,0:T(4,128)(2,1)} %bitcast.2, f32[128]{0:T(128)} %gate_bias_s.1, bf16[128,128]{1,0:T(8,128)(2,1)} %out_weight_s.1, f32[128]{0:T(128)} %out_bias_s.1, ...), custom_call_target="tpu_custom_call" | custom-call | tf_op jit(solution)/shard_map/pallas_call | solution.py:426
  61.1 2.3 %copy.17 = f32[4,512,128]{2,1,0:T(8,128)} copy(f32[4,512,128]{2,1,0:T(8,128)} %shard_map.145) | data formatting | bytes 2097152

commit v5 on v4

--- a/solution.py
+++ b/solution.py
@@ -153,27 +153,40 @@
             for two in (2, 1, 3, 0):
                 if one or two:
                     to = shifted(shifted(at, plane[0], one), plane[1], two)
-                    push(part, to, send_sem.at[chunk, 0], recv_sem.at[chunk, 0])
+                    push(part, to, send_sem.at[chunk, one], recv_sem.at[chunk, one])
 
     along(at, chunk, act)
 
 
-def gather_line(bias, at, chunk, send_sem, recv_sem, spare):
-    wait_for(spare, 15, at, send_sem.at[chunk, 0], recv_sem.at[chunk, 0], False)
+def gather_row(bias, at, chunk, one, send_sem, recv_sem, spare):
+    wait_for(spare, 4 if one else 3, at, send_sem.at[chunk, one], recv_sem.at[chunk, one], False)
 
     def act(line, plane):
-        part = part_of(bias, at, chunk, plane)
+        part = part_of(bias, shifted(at, plane[0], 4 - one), chunk, plane[1:])
         for by in (2, 1, 3):
-            push(part, shifted(at, line, by), send_sem.at[chunk, by], recv_sem.at[chunk, by])
-        push(part, shifted(at, "core", 1), send_sem.at[chunk, 4], recv_sem.at[chunk, 4])
+            push(part, shifted(at, line, by), send_sem.at[chunk, 4 + by], recv_sem.at[chunk, 4 + by])
 
     along(at, chunk, act)
+
+
+def gather_line(bias, at, chunks, send_sem, recv_sem, spare):
+    for one in (0, 1, 3, 2):
+        for chunk in chunks:
+            gather_row(bias, at, chunk, one, send_sem, recv_sem, spare)
+    for chunk in chunks:
+        along(
+            at,
+            chunk,
+            lambda line, plane, chunk=chunk: push(
+                part_of(bias, at, chunk, plane), shifted(at, "core", 1), send_sem.at[chunk, 4], recv_sem.at[chunk, 4]
+            ),
+        )
 
 
 def gather_core(bias, at, chunk, send_sem, recv_sem, spare):
     def act(line, plane):
         for by in (1, 3, 2):
-            wait_for(spare, 16, at, send_sem.at[chunk, by], recv_sem.at[chunk, by], False)
+            wait_for(spare, 16, at, send_sem.at[chunk, 4 + by], recv_sem.at[chunk, 4 + by], False)
             part = part_of(bias, shifted(at, line, 4 - by), chunk, plane)
             push(part, shifted(at, "core", 1), send_sem.at[chunk, 4], recv_sem.at[chunk, 4])
 
@@ -186,7 +199,7 @@
 
 def gather_drain(at, send_sem, recv_sem, spare):
     for chunk in range(4):
-        for phase, count in ((0, 15), (1, 16), (2, 16), (3, 16), (4, 64)):
+        for phase, count in ((0, 3), (1, 4), (2, 4), (3, 4), (4, 64), (5, 16), (6, 16), (7, 16)):
             wait_for(spare, count, at, send_sem.at[chunk, phase], recv_sem.at[chunk, phase], True)
 
 
@@ -326,8 +339,7 @@
         project(i, slice(None), normed[i], proj_s[...], vec(gate_bias_s), query, keys, values, gate)
     for block in range(2):
         pre_scores(block, query, keys, raw)
-    for chunk in range(4):
-        gather_line(bias_s, at, chunk, g_send_s, g_recv_s, recv_a)
+    gather_line(bias_s, at, range(4), g_send_s, g_recv_s, recv_a)
     for block in range(2, 4):
         pre_scores(block, query, keys, raw)
     to_rows, to_slots = perms()
@@ -341,13 +353,12 @@
     def start_step(step, carry):
         block = block_of(at, step)
         here = pl.ds(pl.multiple_of(block * 128, 128), 128)
-        blocks = []
-        for i in range(ROWS):
-            gated = attention_block(i, block, raw, wide, values, gate)
-            update = jnp.dot(gated, out_weight_s[...], preferred_element_type=f32)
-            after = pair[i, here, :] + update + vec(out_bias_s)
-            pair[i, here, :] = after
-            blocks.append(layer_norm(after, vec(gain_e), vec(shift_e)))
+        gated = [attention_block(i, block, raw, wide, values, gate) for i in range(ROWS)]
+        update = jnp.dot(jnp.concatenate(gated, axis=0), out_weight_s[...], preferred_element_type=f32)
+        after = pair[:, here, :].reshape(ROWS * 128, C) + update + vec(out_bias_s)
+        pair[:, here, :] = after.reshape(ROWS, 128, C)
+        ended = layer_norm(after, vec(gain_e), vec(shift_e))
+        blocks = [ended[i * 128 : (i + 1) * 128] for i in range(ROWS)]
         slab = bias_slab(blocks, bias_rows_e[...])
         for s in range(4):
 
@@ -356,7 +367,7 @@
                 bias_e[z, y, x, core, :, s * 128 : (s + 1) * 128] = slab
                 gather_plane(bias_e, at, s, g_send_e, g_recv_e)
                 if s >= 2:
-                    gather_line(bias_e, at, s - 2, g_send_e, g_recv_e, recv_b)
+                    gather_line(bias_e, at, (s - 2,), g_send_e, g_recv_e, recv_b)
 
         send_block(at, step, block, blocks, send_a, recv_a, to_slots, x_send.at[0, step], x_recv.at[0, step])
         return carry
@@ -376,11 +387,11 @@
 
     receive(0)
     receive(1)
-    gather_line(bias_e, at, 2, g_send_e, g_recv_e, recv_b)
-    receive(2)
-    gather_line(bias_e, at, 3, g_send_e, g_recv_e, recv_b)
+    gather_line(bias_e, at, (2,), g_send_e, g_recv_e, recv_b)
     for chunk in (0, 1):
         gather_core(bias_e, at, chunk, g_send_e, g_recv_e, recv_b)
+    receive(2)
+    gather_line(bias_e, at, (3,), g_send_e, g_recv_e, recv_b)
     receive(3)
     for block in range(2):
         pre_scores(block, query, keys, raw)
@@ -444,10 +455,10 @@
             pltpu.VMEM((DEV, 16, C), bf16),
             pltpu.VMEM((DEV, 16, C), bf16),
             pltpu.VMEM((DEV, 16, C), bf16),
-            pltpu.SemaphoreType.DMA((4, 5)),
-            pltpu.SemaphoreType.DMA((4, 5)),
-            pltpu.SemaphoreType.DMA((4, 5)),
-            pltpu.SemaphoreType.DMA((4, 5)),
+            pltpu.SemaphoreType.DMA((4, 8)),
+            pltpu.SemaphoreType.DMA((4, 8)),
+            pltpu.SemaphoreType.DMA((4, 8)),
+            pltpu.SemaphoreType.DMA((4, 8)),
             pltpu.SemaphoreType.DMA((2, 4)),
             pltpu.SemaphoreType.DMA((2, 4)),
             pltpu.SemaphoreType.DMA((4,)),

time: 63.6 us -> 61.9 us (0.973)
  Pallas kernels: 61.1 us -> 59.5 us
    pallas_call x1, Pallas kernels: 61.1 us -> 59.5 us  [body(): pl.pallas_call(kernel, out_shape=jax.ShapeDtypeStruct((ROWS, N, C), f32),...]
where the time goes in v5:
time: 61.9 us; the launch traced here: 61.8 us
  Pallas kernels  59.5 us (96%)
  local copies, waits for them, and re-layouts  2.26 us (4%)
    pallas_call x1, Pallas kernels, body(): pl.pallas_call(kernel, out_shape=jax.ShapeDtypeStruct((ROWS, N, C), f32),...  59.5 us
    unnamed x1, local copies, waits for them, and re-layouts  2.26 us

profile of v5, /device:TPU:1, one launch (start us, length us, event | category | flops | bytes accessed | tf_op | source)
XLA Modules:
  0.0 61.8 jit_solution(9208427042836117717)
XLA Ops:
  0.0 59.5 %shard_map.145 = f32[4,512,128]{2,1,0:T(8,128)} custom-call(f32[4,512,128]{2,1,0:T(8,128)} %pair_hbm.1, f32[128]{0:T(128)} %gain_s.1, f32[128]{0:T(128)} %shift_s.1, bf16[128,512]{1,0:T(8,128)(2,1)} %proj_s.1, bf16[4,128]{1,0:T(4,128)(2,1)} %bitcast.2, f32[128]{0:T(128)} %gate_bias_s.1, bf16[128,128]{1,0:T(8,128)(2,1)} %out_weight_s.1, f32[128]{0:T(128)} %out_bias_s.1, ...), custom_call_target="tpu_custom_call" | custom-call | tf_op jit(solution)/shard_map/pallas_call | solution.py:437
  59.5 2.3 %copy.17 = f32[4,512,128]{2,1,0:T(8,128)} copy(f32[4,512,128]{2,1,0:T(8,128)} %shard_map.145) | data formatting | bytes 2097152

commit v6 on v5

--- a/solution.py
+++ b/solution.py
@@ -388,20 +388,20 @@
     receive(0)
     receive(1)
     gather_line(bias_e, at, (2,), g_send_e, g_recv_e, recv_b)
-    for chunk in (0, 1):
-        gather_core(bias_e, at, chunk, g_send_e, g_recv_e, recv_b)
+    gather_core(bias_e, at, 0, g_send_e, g_recv_e, recv_b)
+    gather_core(bias_e, at, 1, g_send_e, g_recv_e, recv_b)
     receive(2)
     gather_line(bias_e, at, (3,), g_send_e, g_recv_e, recv_b)
-    receive(3)
-    for block in range(2):
-        pre_scores(block, query, keys, raw)
-    gather_core(bias_e, at, 2, g_send_e, g_recv_e, recv_b)
     settle(0)
     settle(1)
-    for block in range(2, 4):
-        pre_scores(block, query, keys, raw)
+    receive(3)
+    pre_scores(0, query, keys, raw)
+    gather_core(bias_e, at, 2, g_send_e, g_recv_e, recv_b)
+    pre_scores(1, query, keys, raw)
+    pre_scores(2, query, keys, raw)
     gather_core(bias_e, at, 3, g_send_e, g_recv_e, recv_b)
     settle(2)
+    pre_scores(3, query, keys, raw)
     settle(3)
 
     def end_step(step, carry):

time: 61.9 us -> 61.1 us (0.987)
  Pallas kernels: 59.5 us -> 58.7 us
    pallas_call x1, Pallas kernels: 59.5 us -> 58.7 us  [body(): pl.pallas_call(kernel, out_shape=jax.ShapeDtypeStruct((ROWS, N, C), f32),...]
where the time goes in v6:
time: 61.1 us; the launch traced here: 60.9 us
  Pallas kernels  58.7 us (96%)
  local copies, waits for them, and re-layouts  2.26 us (4%)
    pallas_call x1, Pallas kernels, body(): pl.pallas_call(kernel, out_shape=jax.ShapeDtypeStruct((ROWS, N, C), f32),...  58.7 us
    unnamed x1, local copies, waits for them, and re-layouts  2.26 us

profile of v6, /device:TPU:1, one launch (start us, length us, event | category | flops | bytes accessed | tf_op | source)
XLA Modules:
  0.0 60.9 jit_solution(10604637884403434860)
XLA Ops:
  0.0 58.7 %shard_map.145 = f32[4,512,128]{2,1,0:T(8,128)} custom-call(f32[4,512,128]{2,1,0:T(8,128)} %pair_hbm.1, f32[128]{0:T(128)} %gain_s.1, f32[128]{0:T(128)} %shift_s.1, bf16[128,512]{1,0:T(8,128)(2,1)} %proj_s.1, bf16[4,128]{1,0:T(4,128)(2,1)} %bitcast.2, f32[128]{0:T(128)} %gate_bias_s.1, bf16[128,128]{1,0:T(8,128)(2,1)} %out_weight_s.1, f32[128]{0:T(128)} %out_bias_s.1, ...), custom_call_target="tpu_custom_call" | custom-call | tf_op jit(solution)/shard_map/pallas_call | solution.py:437
  58.7 2.3 %copy.17 = f32[4,512,128]{2,1,0:T(8,128)} copy(f32[4,512,128]{2,1,0:T(8,128)} %shard_map.145) | data formatting | bytes 2097152

commit v7 on v6

--- a/solution.py
+++ b/solution.py
@@ -344,11 +344,12 @@
         pre_scores(block, query, keys, raw)
     to_rows, to_slots = perms()
     to_lanes[...] = lane_perm()
-    for chunk in range(4):
-        gather_core(bias_s, at, chunk, g_send_s, g_recv_s, recv_a)
-    for chunk in range(4):
-        gather_end(at, chunk, g_send_s, g_recv_s, recv_a)
-        spread_start(bias_s, wide, to_rows, chunk)
+    for chunk in range(5):
+        if chunk < 4:
+            gather_core(bias_s, at, chunk, g_send_s, g_recv_s, recv_a)
+        if chunk > 0:
+            gather_end(at, chunk - 1, g_send_s, g_recv_s, recv_a)
+            spread_start(bias_s, wide, to_rows, chunk - 1)
 
     def start_step(step, carry):
         block = block_of(at, step)

time: 61.1 us -> 62.2 us (1.018)
  Pallas kernels: 58.7 us -> 59.8 us
    pallas_call x1, Pallas kernels: 58.7 us -> 59.8 us  [body(): pl.pallas_call(kernel, out_shape=jax.ShapeDtypeStruct((ROWS, N, C), f32),...]
where the time goes in v7:
time: 62.2 us; the launch traced here: 62 us
  Pallas kernels  59.8 us (96%)
  local copies, waits for them, and re-layouts  2.26 us (4%)
    pallas_call x1, Pallas kernels, body(): pl.pallas_call(kernel, out_shape=jax.ShapeDtypeStruct((ROWS, N, C), f32),...  59.8 us
    unnamed x1, local copies, waits for them, and re-layouts  2.26 us

profile of v7, /device:TPU:1, one launch (start us, length us, event | category | flops | bytes accessed | tf_op | source)
XLA Modules:
  0.0 62.0 jit_solution(4326459145908231036)
XLA Ops:
  0.0 59.8 %shard_map.145 = f32[4,512,128]{2,1,0:T(8,128)} custom-call(f32[4,512,128]{2,1,0:T(8,128)} %pair_hbm.1, f32[128]{0:T(128)} %gain_s.1, f32[128]{0:T(128)} %shift_s.1, bf16[128,512]{1,0:T(8,128)(2,1)} %proj_s.1, bf16[4,128]{1,0:T(4,128)(2,1)} %bitcast.2, f32[128]{0:T(128)} %gate_bias_s.1, bf16[128,128]{1,0:T(8,128)(2,1)} %out_weight_s.1, f32[128]{0:T(128)} %out_bias_s.1, ...), custom_call_target="tpu_custom_call" | custom-call | tf_op jit(solution)/shard_map/pallas_call | solution.py:438
  59.8 2.3 %copy.17 = f32[4,512,128]{2,1,0:T(8,128)} copy(f32[4,512,128]{2,1,0:T(8,128)} %shard_map.145) | data formatting | bytes 2097152
